TPU v7x, 32 devices: a whole 2x2x4 slice. The times are simulated.
32 devices in a mesh: fsdp: 4 (over x, core), seq: 8 (over z, y).
Axes of the slice: x: 2, y: 2, z: 4, core: 2. Of those that a mesh axis runs over, the one named last changes fastest.
Arguments:
- inputs: bfloat16 [96, 6144], P(('fsdp', 'seq')), may hold values from -6 to 6
- out_grad: bfloat16 [96, 6144], P(('fsdp', 'seq')), may hold values from -6 to 6
- first_tiles: bfloat16 [8, 208, 4096], P('seq', 'fsdp'), may hold values from -0.15625 to 0.15625
- first_count: int32 [8, 4], P('seq'), may hold values from 1 to 52, 192 in all within a row
- first_blocks: int32 [8, 192], P('seq'), may hold values from 0 to 767, as said below
- second_tiles: bfloat16 [8, 208, 4096], P('seq', 'fsdp'), may hold values from -0.109375 to 0.109375
- second_count: int32 [8, 4], P('seq'), may hold values from 1 to 52, 192 in all within a row
- second_blocks: int32 [8, 192], P('seq'), may hold values from 0 to 767, as said below
Outputs:
- output: bfloat16 [96, 6144], P(('fsdp', 'seq'))
- in_grad: bfloat16 [96, 6144], P(('fsdp', 'seq'))
Inputs may be any that keep to these rules, and one draw needn't show every extreme that they name: Each row of first_blocks lists 192 different blocks of 0 to 767, and holds both 0 and 767. Each row of second_blocks lists 192 different blocks of 0 to 767, and holds both 0 and 767. `first_count`: each row sums to 192, and its largest count is 52. `second_count`: each row sums to 192, and its largest count is 52.
All inputs are finite; a program needn't handle non-finite values.
Results may differ from a plain program's by a relative error of at most 0.0051.
Values may be sent and summed in bfloat16 or wider, within the bound.
A program may use at most 128 MiB of HBM per device.

v0:
```python
import jax
import jax.numpy as jnp
from jax import lax
from jax.sharding import PartitionSpec as P

BS = 64
HB_DEV = 8


def gelu_pair(hidden):
    inner = 0.7978845608 * (hidden + 0.044715 * hidden * hidden * hidden)
    tangent = jnp.tanh(inner)
    value = 0.5 * hidden * (1.0 + tangent)
    slope = 0.5 * (1.0 + tangent) + 0.5 * hidden * (1.0 - tangent * tangent) * 0.7978845608 * (
        1.0 + 3.0 * 0.044715 * hidden * hidden
    )
    return (value, slope)


def entry_slots(counts, kept, capacity):
    ends = jnp.cumsum(counts, dtype=jnp.int32)
    starts = ends - counts
    entry = jnp.arange(kept, dtype=jnp.int32)
    owner = jnp.sum((entry[:, None] >= ends[None, :]).astype(jnp.int32), axis=1, dtype=jnp.int32)
    onehot = (owner[:, None] == jnp.arange(counts.shape[0], dtype=jnp.int32)[None, :]).astype(
        jnp.int32
    )
    first = jnp.sum(onehot * starts[None, :], axis=1, dtype=jnp.int32)
    return owner * capacity + entry - first


def slot_entries(slots, counts, blocks, capacity):
    kept = blocks.shape[0]
    ends = jnp.cumsum(counts, dtype=jnp.int32)
    starts = ends - counts
    owner = slots // capacity
    within = slots % capacity
    onehot = (owner[:, None] == jnp.arange(counts.shape[0], dtype=jnp.int32)[None, :]).astype(
        jnp.int32
    )
    owned = jnp.sum(onehot * counts[None, :], axis=1, dtype=jnp.int32)
    first = jnp.sum(onehot * starts[None, :], axis=1, dtype=jnp.int32)
    live = within < owned
    entry = jnp.clip(first + within, 0, kept - 1)
    pick = (entry[:, None] == jnp.arange(kept, dtype=jnp.int32)[None, :]).astype(jnp.int32)
    block = jnp.sum(pick * blocks[None, :], axis=1, dtype=jnp.int32)
    return (block, live)


def place_second(grid, tiles, block, live, width_blocks):
    number = tiles.shape[0]
    hid_block = jnp.where(live, block // width_blocks, HB_DEV)
    col_block = block % width_blocks
    return grid.at[hid_block, :, col_block, :].set(tiles.reshape(number, BS, BS), mode="drop")


def on_device(
    inputs,
    out_grad,
    first_tiles,
    first_count,
    first_blocks,
    second_tiles,
    second_count,
    second_blocks,
):
    rows_in, rows_grad = (
        lax.all_gather(inputs, "seq", axis=0, tiled=True),
        lax.all_gather(out_grad, "seq", axis=0, tiled=True),
    )
    width = rows_in.shape[1]
    width_blocks = width // BS
    capacity = first_tiles.shape[1]
    list_one = first_blocks[0]
    list_two = second_blocks[0]
    counts_one = first_count[0]
    counts_two = second_count[0]
    kept = list_one.shape[0]
    whole_one = lax.all_gather(first_tiles, "fsdp", axis=1, tiled=True)[0]
    chosen_one = whole_one[entry_slots(counts_one, kept, capacity)].reshape(kept, BS, BS)
    grid_one = jnp.zeros((width_blocks, BS, HB_DEV, BS), jnp.bfloat16)
    grid_one = grid_one.at[list_one // HB_DEV, :, list_one % HB_DEV, :].set(chosen_one)
    first = grid_one.reshape(width, HB_DEV * BS)
    hidden = jnp.dot(rows_in, first, preferred_element_type=jnp.float32)
    value, slope = gelu_pair(hidden)
    acts = value.astype(jnp.bfloat16)
    empty = jnp.zeros((HB_DEV, BS, width_blocks, BS), jnp.bfloat16)
    piece = lax.all_gather(second_tiles, "fsdp", axis=1, tiled=True)
    slots = jnp.arange(piece.shape[1], dtype=jnp.int32)
    block, live = slot_entries(slots, counts_two, list_two, capacity)
    grid_two = place_second(empty, piece[0], block, live, width_blocks)
    second = grid_two.reshape(HB_DEV * BS, width)
    total_out = jnp.dot(acts, second, preferred_element_type=jnp.float32)
    back = lax.dot_general(
        rows_grad, second, (((1,), (1,)), ((), ())), preferred_element_type=jnp.float32
    )
    pre_grad = (back * slope).astype(jnp.bfloat16)
    out_part = lax.psum_scatter(total_out, "seq", scatter_dimension=0, tiled=True)
    grad_part = lax.psum_scatter(
        lax.dot_general(
            pre_grad, first, (((1,), (1,)), ((), ())), preferred_element_type=jnp.float32
        ),
        "seq",
        scatter_dimension=0,
        tiled=True,
    )
    return (out_part.astype(jnp.bfloat16), grad_part.astype(jnp.bfloat16))


def solution(mesh):
    placed = (
        P(("fsdp", "seq"), None),
        P(("fsdp", "seq"), None),
        P("seq", "fsdp", None),
        P("seq", None),
        P("seq", None),
        P("seq", "fsdp", None),
        P("seq", None),
        P("seq", None),
    )
    return jax.shard_map(
        on_device,
        mesh=mesh,
        in_specs=placed,
        out_specs=(P(("fsdp", "seq"), None), P(("fsdp", "seq"), None)),
        check_vma=False,
    )
```

profile of v0, /device:TPU:0, one launch (start us, length us, event | category | flops | bytes accessed | tf_op | source)
XLA Modules:
  0.0 336.5 jit_solution(2227274284606166976)
XLA Ops:
  7.2 0.0 copy-start.6
  7.2 0.0 copy-start.4
  7.2 0.0 copy-start.5
  7.2 0.0 copy-start.2
  7.2 0.0 copy-start.3
  7.2 0.0 all-gather.7.cloned.1.call-start
  7.3 2.9 copy.36
  10.1 0.0 all-gather.7.cloned.1.call-update
  10.2 0.0 all-gather.5.cloned.1.call-start
  10.2 2.9 copy.32
  13.1 0.0 all-gather.5.cloned.1.call-update
  13.1 0.8 reduce-window_1_clone.1
  14.0 0.8 reduce-window.6
  14.8 0.1 convert_reduce_fusion
  14.9 33.0 %all-gather = bf16[8,3,6144]{2,1,0:T(4,128)(2,1)S(1)} all-gather(bf16[1,3,6144]{2,1,0:T(4,128)(2,1)} %bitcast.66), channel_id=1, replica_groups=mesh['fsdp'=4,'seq'=8] {'seq'}, dimensions={0}, use_global_device_ids=true | all-gather | bytes 331776 | tf_op jit(solution)/shard_map/all_gather | solution.py:68
  47.9 1.0 reshape.326
  48.8 31.2 %all-gather.1 = bf16[8,3,6144]{2,1,0:T(4,128)(2,1)S(1)} all-gather(bf16[1,3,6144]{2,1,0:T(4,128)(2,1)} %bitcast.67), channel_id=1, replica_groups=mesh['fsdp'=4,'seq'=8] {'seq'}, dimensions={0}, use_global_device_ids=true | all-gather | bytes 331776 | tf_op jit(solution)/shard_map/all_gather | solution.py:69
  80.0 1.0 reshape.328
  81.0 0.0 copy-done.6
  81.0 0.6 dynamic-slice
  82.3 0.0 copy-done.5
  82.3 0.1 select_reduce_fusion.3
  82.4 0.0 copy-done.4
  82.4 0.1 select_reduce_fusion.2
  82.6 0.0 copy-done.2
  82.6 0.1 select_reduce_fusion
  82.7 0.0 copy-done.3
  82.8 0.0 all-gather.7.cloned.1.call-done
  82.8 8.2 %copy.37 = bf16[1,208,4096]{1,2,0:T(8,128)(2,1)} copy(bf16[1,208,4096]{2,0,1:T(2,128)(2,1)} %all-gather.7.cloned.1.call-done) | data formatting | bytes 3407872 | tf_op jit(solution)/shard_map/all_gather | solution.py:88
  91.0 4.5 %copy.38 = bf16[208,64,64]{2,1,0:T(8,128)(2,1)S(1)} copy(bf16[208,64,64]{0,2,1:T(8,128)(2,1)} %bitcast.65) | data formatting | bytes 3407872 | tf_op jit(solution)/shard_map/reshape;squeeze | solution.py:54
  95.4 7.7 %broadcast_in_dim.8 = bf16[8,64,96,64]{3,1,2,0:T(8,128)(2,1)} broadcast(bf16[]{:T(256)} %constant.74.clone.1), dimensions={} | broadcast | bytes 6291458 | tf_op jit(solution)/shard_map/broadcast_in_dim | solution.py:87
  103.1 27.7 %scatter_fusion.1 = bf16[8,64,96,64]{3,1,2,0:T(8,128)(2,1)} fusion(bf16[8,64,96,64]{3,1,2,0:T(8,128)(2,1)} %broadcast_in_dim.8, s32[208]{0:T(256)S(1)} %bitcast.62, bf16[208,64,64]{2,1,0:T(8,128)(2,1)S(1)} %copy.38), kind=kCustom, calls=%fused_computation.2 | custom fusion | bytes 5113472 | tf_op jit(solution)/shard_map/scatter | solution.py:54
  130.8 14.6 %copy.39 = bf16[8,64,96,64]{3,2,1,0:T(8,128)(2,1)} copy(bf16[8,64,96,64]{3,1,2,0:T(8,128)(2,1)} %scatter_fusion.1) | data formatting | bytes 12582912 | tf_op jit(solution)/shard_map/scatter | solution.py:54
  145.3 16.9 %reshape.304 = bf16[512,6144]{1,0:T(8,128)(2,1)} reshape(bf16[8,64,96,64]{3,2,1,0:T(8,128)(2,1)} %copy.39) | data formatting | bytes 12582912 | tf_op jit(solution)/shard_map/reshape | solution.py:92
  162.3 3.8 %copy.42 = bf16[1,208,4096]{2,1,0:T(8,128)(2,1)S(1)} copy(bf16[1,208,4096]{2,0,1:T(2,128)(2,1)} %all-gather.5.cloned.1.call-done) | data formatting | bytes 3407872
  166.1 1.5 gather_fusion
  167.6 2.5 copy.33
  170.1 4.2 %copy.34 = bf16[192,64,64]{2,1,0:T(8,128)(2,1)S(1)} copy(bf16[192,64,64]{0,2,1:T(8,128)(2,1)} %bitcast.64) | data formatting | bytes 3145728 | tf_op jit(solution)/shard_map/reshape | solution.py:80
  174.3 7.7 %broadcast_in_dim.7 = bf16[96,64,8,64]{3,1,2,0:T(8,128)(2,1)} broadcast(bf16[]{:T(256)} %constant.74.clone.1), dimensions={} | broadcast | bytes 6291458 | tf_op jit(solution)/shard_map/broadcast_in_dim | solution.py:81
  182.0 25.7 %scatter_fusion = bf16[96,64,8,64]{3,1,2,0:T(8,128)(2,1)} fusion(bf16[96,64,8,64]{3,1,2,0:T(8,128)(2,1)} %broadcast_in_dim.7, s32[192]{0:T(256)S(1)} %bitcast.63, bf16[192,64,64]{2,1,0:T(8,128)(2,1)S(1)} %copy.34), kind=kCustom, calls=%fused_computation.1 | custom fusion | bytes 4720128 | tf_op jit(solution)/shard_map/scatter | solution.py:82
  207.7 15.7 %copy.35 = bf16[96,64,8,64]{3,2,1,0:T(8,128)(2,1)} copy(bf16[96,64,8,64]{3,1,2,0:T(8,128)(2,1)} %scatter_fusion) | data formatting | bytes 12582912 | tf_op jit(solution)/shard_map/scatter | solution.py:82
  223.5 17.2 %reshape.303 = bf16[6144,512]{1,0:T(8,128)(2,1)} reshape(bf16[96,64,8,64]{3,2,1,0:T(8,128)(2,1)} %copy.35) | data formatting | bytes 12582912 | tf_op jit(solution)/shard_map/reshape | solution.py:83
  240.7 3.7 %convolution_bitcast_fusion.1 = f32[24,512]{1,0:T(8,128)S(1)} fusion(bf16[6144,512]{1,0:T(8,128)(2,1)} %reshape.303, bf16[24,6144]{1,0:T(8,128)(2,1)S(1)} %copy-done), kind=kOutput, calls=%fused_computation.6 | convolution fusion | flops 150994944 | bytes 6635520 | tf_op jit(solution)/shard_map/dot_general | solution.py:84
  244.4 3.7 %fusion.17 = f32[24,6144]{1,0:T(8,128)S(1)} fusion(bf16[512,6144]{1,0:T(8,128)(2,1)} %reshape.304, f32[24,512]{1,0:T(8,128)S(1)} %convolution_bitcast_fusion.1), kind=kOutput, calls=%fused_computation.28 | convolution fusion | flops 151105536 | bytes 6930432 | tf_op jit(solution)/shard_map/dot_general | solution.py:93
  248.1 0.0 copy-done.1
  248.1 8.0 %fusion.2 = f32[24,6144]{1,0:T(8,128)S(1)} fusion(bf16[6144,512]{1,0:T(8,128)(2,1)} %reshape.303, bf16[512,6144]{1,0:T(8,128)(2,1)} %reshape.304, bf16[24,6144]{1,0:T(8,128)(2,1)S(1)} %copy-done.1, f32[24,512]{1,0:T(8,128)S(1)} %convolution_bitcast_fusion.1), kind=kOutput, calls=%fused_computation.8 | convolution fusion | flops 302223360 | bytes 13516800 | tf_op jit(solution)/shard_map/dot_general | solution.py:100
  256.2 72.8 %all-reduce.4 = (bf16[24,6144]{1,0:T(8,128)(2,1)S(1)}, bf16[24,6144]{1,0:T(8,128)(2,1)S(1)}) all-reduce(f32[24,6144]{1,0:T(8,128)S(1)} %fusion.17, f32[24,6144]{1,0:T(8,128)S(1)} %fusion.2), channel_id=2, replica_groups=mesh['fsdp'=4,'seq'=8] {'seq'}, use_global_device_ids=true, to_apply=%region_9.10.clone | all-reduce | flops 294912 | bytes 1769472
  328.9 0.7 dynamic-slice_convert_fusion
  (15 shorter events, 0.1 us)
Async XLA Ops:
  7.2 73.9 %copy-start.6 = (u32[32]{0:T(128)S(1)}, u32[32]{0:T(128)}, u32[]{:S(2)}) copy-start(u32[32]{0:T(128)} %constant.132) | copy-start | bytes 388
  7.2 75.3 %copy-start.4 = (s32[1,4]{1,0:T(1,128)S(1)}, s32[1,4]{1,0:T(1,128)}, u32[]{:S(2)}) copy-start(s32[1,4]{1,0:T(1,128)} %param.14) | copy-start | bytes 52
  7.2 75.1 %copy-start.5 = (s32[1,4]{1,0:T(1,128)S(1)}, s32[1,4]{1,0:T(1,128)}, u32[]{:S(2)}) copy-start(s32[1,4]{1,0:T(1,128)} %param.11) | copy-start | bytes 52
  7.2 75.4 %copy-start.2 = (s32[1,192]{1,0:T(1,128)S(1)}, s32[1,192]{1,0:T(1,128)}, u32[]{:S(2)}) copy-start(s32[1,192]{1,0:T(1,128)} %param.15) | copy-start | bytes 2308
  7.2 75.5 %copy-start.3 = (s32[1,192]{1,0:T(1,128)S(1)}, s32[1,192]{1,0:T(1,128)}, u32[]{:S(2)}) copy-start(s32[1,192]{1,0:T(1,128)} %param.12) | copy-start | bytes 2308
  7.2 75.6 %all-gather.7.cloned.1.call-start = ((), (), s32[]{:S(2)}) async-start(), calls=%async_computation.1 | async-start | bytes 4259840 | tf_op jit(solution)/shard_map/all_gather | solution.py:88
  10.2 152.1 %all-gather.5.cloned.1.call-start = ((), (), s32[]{:S(2)}) async-start(), calls=%async_computation | async-start | bytes 4259840 | tf_op jit(solution)/shard_map/all_gather | solution.py:79
  223.5 17.2 %copy-start = (bf16[24,6144]{1,0:T(8,128)(2,1)S(1)}, bf16[24,6144]{1,0:T(8,128)(2,1)}, u32[]{:S(2)}) copy-start(bf16[24,6144]{1,0:T(8,128)(2,1)} %reshape.326) | copy-start | bytes 884740
  240.7 7.5 %copy-start.1 = (bf16[24,6144]{1,0:T(8,128)(2,1)S(1)}, bf16[24,6144]{1,0:T(8,128)(2,1)}, u32[]{:S(2)}) copy-start(bf16[24,6144]{1,0:T(8,128)(2,1)} %reshape.328) | copy-start | bytes 884740
Sparse Core Ops, SparseCore 0:
  10.3 32.7 all-gather.6
  44.6 30.0 all-gather.4
where the time goes:
time: 340 us; the launch traced here: 336 us
  local copies, waits for them, and re-layouts  167 us (49%)
  blocking collectives  137 us (40%)
  matrix products  15.5 us (5%)
  between operations  14.9 us (4%)
    unnamed x1, blocking collectives  72.8 us
    scatter x2, local copies, waits for them, and re-layouts, place_second(): grid.at[hid_block, :, col_block, :]  42.2 us
    scatter x2, local copies, waits for them, and re-layouts, on_device(): grid_one.at[list_one // HB_DEV, :, list_one % HB_DEV, :].set(chosen_one)  41.4 us
    all_gather x1, blocking collectives, on_device(): lax.all_gather(inputs, 'seq', axis=0, tiled=True)  33 us
    all_gather x1, blocking collectives, on_device(): lax.all_gather(out_grad, 'seq', axis=0, tiled=True)  31.2 us
    reshape x1, local copies, waits for them, and re-layouts, on_device(): first = grid_one.reshape(width, HB_DEV * BS)  17.2 us
    reshape x1, local copies, waits for them, and re-layouts, on_device(): second = grid_two.reshape(HB_DEV * BS, width)  16.9 us
    unnamed x20, local copies, waits for them, and re-layouts  12.2 us
  transfers between devices with their start and end apart: 2, of which 0 were waited for; matrix products, arithmetic and copies ran while one was open for 26% of the time, Pallas kernels for 0%

commit v1 on v0

v1 whole, which is shorter than its diff:
```python
import functools

import jax
import jax.numpy as jnp
from jax import lax
from jax.experimental import pallas as pl
from jax.experimental.pallas import tpu as pltpu
from jax.sharding import PartitionSpec as P

BS = 64
HB_DEV = 8
HALF = BS // 2
LANES = 128
MESH = pl.DeviceIdType.MESH
F32 = jnp.float32
BF16 = jnp.bfloat16


def gelu_pair(hidden):
    inner = 0.7978845608 * (hidden + 0.044715 * hidden * hidden * hidden)
    tangent = jnp.tanh(inner)
    value = 0.5 * hidden * (1.0 + tangent)
    slope = 0.5 * (1.0 + tangent) + 0.5 * hidden * (1.0 - tangent * tangent) * 0.7978845608 * (
        1.0 + 3.0 * 0.044715 * hidden * hidden
    )
    return (value, slope)


def block_slots(counts, blocks, capacity, number):
    shards = counts.shape[1]
    kept = blocks.shape[1]
    zero = shards * capacity
    shard = jnp.arange(shards, dtype=jnp.int32)
    ends = jnp.sum(jnp.where(shard[:, None] <= shard[None, :], counts[:, :, None], 0), axis=1)
    entry = jnp.arange(kept, dtype=jnp.int32)
    past = entry[None, :, None] >= ends[:, None, :]
    slot = entry[None, :] + jnp.sum(jnp.where(past, capacity - counts[:, None, :], 0), axis=2)
    block = jnp.arange(number, dtype=jnp.int32)
    same = blocks[:, None, :] == block[None, :, None]
    return zero + jnp.sum(jnp.where(same, slot[:, None, :] - zero, 0), axis=2)


def natural(position):
    within = position % BS
    return position - within + 2 * (within % HALF) + within // HALF


def kernel(
    n_fsdp,
    n_seq,
    slots_ref,
    x_ref,
    g_ref,
    one_ref,
    two_ref,
    out_ref,
    grad_ref,
    tiles_one,
    tiles_two,
    stage,
    first,
    second,
    own_rows,
    got_x,
    got_g,
    spread,
    mat_x,
    mat_g,
    send_out,
    send_grad,
    got_out,
    got_grad,
    tile_send,
    tile_recv,
    row_send,
    row_recv,
    sum_send,
    sum_recv,
):
    capacity = one_ref.shape[1]
    own, width = x_ref.shape
    groups = width // LANES
    rows = own * n_seq
    chunk = own * groups
    width_blocks = width // BS
    hid = HB_DEV * BS
    zero_slot = n_fsdp * capacity
    f = lax.axis_index("fsdp")
    s = lax.axis_index("seq")
    pair = f + 1 - 2 * lax.rem(f, 2)
    others = [lax.rem(f + 2 * j, n_fsdp) for j in range(1, n_fsdp // 2)]
    pair_others = [lax.rem(pair + 2 * j, n_fsdp) for j in range(1, n_fsdp // 2)]
    peers = [lax.rem(s + j, n_seq) for j in range(1, n_seq)]

    barrier = pltpu.get_barrier_semaphore()
    for peer in [pair] + others:
        pl.semaphore_signal(barrier, inc=1, device_id=(peer, s), device_id_type=MESH)
    for peer in peers:
        pl.semaphore_signal(barrier, inc=1, device_id=(f, peer), device_id_type=MESH)

    def lay_tiles(source, target):
        for j in range(HALF):
            piece = source[0, :, j * LANES:(j + 1) * LANES].astype(F32)
            stage[pl.ds(j, capacity, stride=HALF), :] = piece
        target[pl.ds(f * capacity, capacity)] = (
            stage[0:capacity * HALF, :].astype(BF16).reshape(capacity, HALF, LANES)
        )
        target[zero_slot] = jnp.zeros((HALF, LANES), BF16)

    def tile_copy(which, buffer, owner, target, sem):
        part = buffer.at[pl.ds(owner * capacity, capacity)]
        return pltpu.make_async_remote_copy(
            src_ref=part,
            dst_ref=part,
            send_sem=tile_send.at[which, sem],
            recv_sem=tile_recv.at[which, owner],
            device_id=(target, s),
            device_id_type=MESH,
        )

    def row_copy(which, source, got, owner, target, sem):
        return pltpu.make_async_remote_copy(
            src_ref=source,
            dst_ref=got.at[owner],
            send_sem=row_send.at[which, sem],
            recv_sem=row_recv.at[which, owner],
            device_id=(f, target),
            device_id_type=MESH,
        )

    def sum_copy(which, source, got, owner, target, sem):
        return pltpu.make_async_remote_copy(
            src_ref=source.at[target],
            dst_ref=got.at[owner],
            send_sem=sum_send.at[which, sem],
            recv_sem=sum_recv.at[which, owner],
            device_id=(f, target),
            device_id_type=MESH,
        )

    sent = []

    def start(copy):
        copy.start()
        sent.append(copy)

    position = lax.broadcasted_iota(jnp.int32, (LANES, LANES), 1)
    row = lax.broadcasted_iota(jnp.int32, (LANES, LANES), 0)
    to_halves = jnp.where(natural(position) == row, 1.0, 0.0).astype(BF16)
    from_halves = jnp.where(natural(row) == position, 1.0, 0.0).astype(BF16)

    lay_tiles(one_ref, tiles_one)
    pl.semaphore_wait(barrier, 1 + len(others) + len(peers))
    for j, peer in enumerate(others):
        start(tile_copy(0, tiles_one, f, peer, j))

    def lay_rows(source):
        for k in range(groups):
            piece = source[:, k * LANES:(k + 1) * LANES].astype(F32)
            stage[pl.ds(k, own, stride=groups), :] = piece
        return stage[0:chunk, :].astype(BF16)

    own_rows[0] = jnp.dot(lay_rows(x_ref), to_halves, preferred_element_type=F32).astype(BF16)
    for j, peer in enumerate(peers):
        start(row_copy(0, own_rows.at[0], got_x, s, peer, j))
    start(tile_copy(0, tiles_one, f, pair, n_fsdp))
    lay_tiles(two_ref, tiles_two)
    for j, peer in enumerate(others):
        start(tile_copy(1, tiles_two, f, peer, j))
    own_rows[1] = lay_rows(g_ref)
    for j, peer in enumerate(peers):
        start(row_copy(1, own_rows.at[1], got_g, s, peer, j))
    start(tile_copy(1, tiles_two, f, pair, n_fsdp))
    got_x[s] = own_rows[0]
    got_g[s] = own_rows[1]

    def collect_rows(which, got, mat):
        for peer in peers:
            row_copy(which, own_rows.at[which], got, peer, peer, 0).wait_recv()
        spread[...] = got[...].reshape(n_seq * chunk, LANES).astype(F32)
        for k in range(groups):
            piece = spread[pl.ds(k, rows, stride=groups), :]
            mat[:, k * LANES:(k + 1) * LANES] = piece.astype(BF16)

    def collect_tiles(which, buffer):
        for j, peer in enumerate(others):
            tile_copy(which, buffer, peer, pair, 0).wait_recv()
            start(tile_copy(which, buffer, peer, pair, n_fsdp + 1 + j))
        tile_copy(which, buffer, pair, pair, 0).wait_recv()
        for peer in pair_others:
            tile_copy(which, buffer, peer, pair, 0).wait_recv()

    def joined(buffer, left, right):
        a = buffer[left]
        b = buffer[right]
        even = jnp.concatenate([a[:, :BS], b[:, :BS]], axis=1)
        odd = jnp.concatenate([a[:, BS:], b[:, BS:]], axis=1)
        return jnp.concatenate([even, odd], axis=0)

    collect_rows(0, got_x, mat_x)
    collect_tiles(0, tiles_one)

    step = 4

    def build_first(i, total):
        for r in range(step):
            block = (i * step + r) * HB_DEV
            at = pl.ds(pl.multiple_of((i * step + r) * BS, BS), BS)
            for j in range(HB_DEV // 2):
                tile = joined(
                    tiles_one, slots_ref[0, block + 2 * j], slots_ref[0, block + 2 * j + 1]
                )
                first[at, j * LANES:(j + 1) * LANES] = tile
        at = pl.ds(pl.multiple_of(i * (step * BS), step * BS), step * BS)
        return total + jnp.dot(mat_x[:, at], first[at, :], preferred_element_type=F32)

    hidden = lax.fori_loop(
        0, width_blocks // step, build_first, jnp.zeros((rows, hid), F32)
    )

    def reorder(value, matrix):
        parts = [
            jnp.dot(value[:, k * LANES:(k + 1) * LANES], matrix, preferred_element_type=F32)
            for k in range(hid // LANES)
        ]
        return jnp.concatenate(parts, axis=1)

    top = hidden.astype(BF16)
    rest = (hidden - top.astype(F32)).astype(BF16)
    hidden = reorder(top, to_halves) + reorder(rest, to_halves)
    value, slope = gelu_pair(hidden)
    acts = value.astype(BF16)

    collect_rows(1, got_g, mat_g)
    collect_tiles(1, tiles_two)

    def build_second(i, total):
        for k in range(2):
            block = i * 4 + 2 * k
            at = pl.ds(pl.multiple_of((2 * i + k) * LANES, LANES), LANES)
            for r in range(HB_DEV):
                left = r * width_blocks + block
                tile = joined(tiles_two, slots_ref[1, left], slots_ref[1, left + 1])
                second[r * BS:(r + 1) * BS, at] = tile
        at = pl.ds(pl.multiple_of(2 * i * LANES, 2 * LANES), 2 * LANES)
        weight = second[:, at]
        part = jnp.dot(acts, weight, preferred_element_type=F32)
        for k in range(2):
            spread[pl.ds(2 * i + k, rows, stride=groups), :] = part[:, k * LANES:(k + 1) * LANES]
        return total + lax.dot_general(
            mat_g[:, at], weight, (((1,), (1,)), ((), ())), preferred_element_type=F32
        )

    back = lax.fori_loop(0, groups // 2, build_second, jnp.zeros((rows, hid), F32))
    send_out[...] = spread[...].astype(BF16).reshape(n_seq, chunk, LANES)
    for j, peer in enumerate(peers):
        start(sum_copy(0, send_out, got_out, s, peer, j))

    pre = (back * slope).astype(BF16)
    pre = reorder(pre, from_halves).astype(BF16)

    def in_grad(i, carry):
        at = pl.ds(pl.multiple_of(2 * i * LANES, 2 * LANES), 2 * LANES)
        part = lax.dot_general(
            pre, first[at, :], (((1,), (1,)), ((), ())), preferred_element_type=F32
        )
        for k in range(2):
            spread[pl.ds(2 * i + k, rows, stride=groups), :] = part[:, k * LANES:(k + 1) * LANES]
        return carry

    lax.fori_loop(0, groups // 2, in_grad, 0)
    send_grad[...] = spread[...].astype(BF16).reshape(n_seq, chunk, LANES)
    for j, peer in enumerate(peers):
        start(sum_copy(1, send_grad, got_grad, s, peer, j))

    def finish(which, source, got, target):
        got[s] = source[s]
        for peer in peers:
            sum_copy(which, source, got, peer, peer, 0).wait_recv()
        total = lax.fori_loop(
            0, n_seq, lambda i, t: t + got[i].astype(F32), jnp.zeros((chunk, LANES), F32)
        )
        if which == 1:
            total = jnp.dot(total.astype(BF16), from_halves, preferred_element_type=F32)
        stage[0:chunk, :] = total
        for k in range(groups):
            piece = stage[pl.ds(k, own, stride=groups), :]
            target[:, k * LANES:(k + 1) * LANES] = piece.astype(BF16)

    finish(0, send_out, got_out, out_ref)
    finish(1, send_grad, got_grad, grad_ref)
    for copy in sent:
        copy.wait_send()


def on_device(
    n_fsdp,
    n_seq,
    inputs,
    out_grad,
    first_tiles,
    first_count,
    first_blocks,
    second_tiles,
    second_count,
    second_blocks,
):
    own, width = inputs.shape
    capacity = first_tiles.shape[1]
    width_blocks = width // BS
    rows = own * n_seq
    chunk = own * (width // LANES)
    hid = HB_DEV * BS
    table = block_slots(
        jnp.concatenate([first_count, second_count]),
        jnp.concatenate([first_blocks, second_blocks]),
        capacity,
        width_blocks * HB_DEV,
    )
    vmem = pl.BlockSpec(memory_space=pltpu.VMEM)
    bank = pltpu.VMEM((n_fsdp * capacity + 1, HALF, LANES), BF16)
    every = pltpu.VMEM((n_seq, chunk, LANES), BF16)
    return pl.pallas_call(
        functools.partial(kernel, n_fsdp, n_seq),
        out_shape=(
            jax.ShapeDtypeStruct((own, width), BF16),
            jax.ShapeDtypeStruct((own, width), BF16),
        ),
        in_specs=[pl.BlockSpec(memory_space=pltpu.SMEM)] + [vmem] * 4,
        out_specs=(vmem, vmem),
        scratch_shapes=[
            bank,
            bank,
            pltpu.VMEM((max(capacity * HALF, chunk), LANES), F32),
            pltpu.VMEM((width, hid), BF16),
            pltpu.VMEM((hid, width), BF16),
            pltpu.VMEM((2, chunk, LANES), BF16),
            every,
            every,
            pltpu.VMEM((n_seq * chunk, LANES), F32),
            pltpu.VMEM((rows, width), BF16),
            pltpu.VMEM((rows, width), BF16),
            every,
            every,
            every,
            every,
            pltpu.SemaphoreType.DMA((2, n_fsdp + n_fsdp // 2)),
            pltpu.SemaphoreType.DMA((2, n_fsdp)),
            pltpu.SemaphoreType.DMA((2, n_seq)),
            pltpu.SemaphoreType.DMA((2, n_seq)),
            pltpu.SemaphoreType.DMA((2, n_seq)),
            pltpu.SemaphoreType.DMA((2, n_seq)),
        ],
        compiler_params=pltpu.CompilerParams(
            collective_id=0, has_side_effects=True, vmem_limit_bytes=56 * 1024 * 1024
        ),
    )(table, inputs, out_grad, first_tiles, second_tiles)


def solution(mesh):
    placed = (
        P(("fsdp", "seq"), None),
        P(("fsdp", "seq"), None),
        P("seq", "fsdp", None),
        P("seq", None),
        P("seq", None),
        P("seq", "fsdp", None),
        P("seq", None),
        P("seq", None),
    )
    return jax.shard_map(
        functools.partial(on_device, mesh.shape["fsdp"], mesh.shape["seq"]),
        mesh=mesh,
        in_specs=placed,
        out_specs=(P(("fsdp", "seq"), None), P(("fsdp", "seq"), None)),
        check_vma=False,
    )
```

time: 340 us -> 58.5 us (0.17)
  local copies, waits for them, and re-layouts: 167 us -> 2.87 us
  blocking collectives: 137 us -> 0 us
  Pallas kernels: 0 us -> 52.4 us
  matrix products: 15.5 us -> 0 us
  between operations: 14.9 us -> 0.65 us
    scatter x4 -> x0, local copies, waits for them, and re-layouts: 83.6 us -> none  [the longest x2 42.2 us: place_second(): grid.at[hid_block, :, col_block, :]]
    unnamed x1 -> x0, blocking collectives: 72.8 us -> none
    all_gather x2 -> x0, blocking collectives: 64.2 us -> none  [the longest x1 33 us: on_device(): lax.all_gather(inputs, 'seq', axis=0, tiled=True)]
    pallas_call x0 -> x1, Pallas kernels: none -> 52.4 us  [on_device(): pl.pallas_call(functools.partial(kernel, n_fsdp, n_seq), out_shape=(jax.S...]
    reshape x3 -> x0, local copies, waits for them, and re-layouts: 38.3 us -> none  [the longest x1 17.2 us: on_device(): first = grid_one.reshape(width, HB_DEV * BS)]
    dot_general x3 -> x0, matrix products: 15.5 us -> none  [the longest x1 8.03 us: on_device(): lax.dot_general(pre_grad, first, (((1,), (1,)), ((), ())), preferred_elem...]
    broadcast_in_dim x2 -> x0, local copies, waits for them, and re-layouts: 15.4 us -> none  [the longest x1 7.69 us: on_device(): empty = jnp.zeros((HB_DEV, BS, width_blocks, BS), jnp.bfloat16)]
    unnamed x20 -> x2, local copies, waits for them, and re-layouts: 12.2 us -> 2.87 us
  transfers between devices with their start and end apart: 2 -> 0, of which waited for: 0 -> 0; matrix products, arithmetic and copies ran while one was open for 26% -> 0% of each run, Pallas kernels for 0% -> 0%
where the time goes in v1:
time: 58.5 us; the launch traced here: 58.3 us
  Pallas kernels  52.4 us (90%)
  local copies, waits for them, and re-layouts  2.87 us (5%)
  other arithmetic  2.37 us (4%)
  between operations  0.65 us (1%)
    pallas_call x1, Pallas kernels, on_device(): pl.pallas_call(functools.partial(kernel, n_fsdp, n_seq), out_shape=(jax.S...  52.4 us
    unnamed x2, local copies, waits for them, and re-layouts  2.87 us

profile of v1, /device:TPU:0, one launch (start us, length us, event | category | flops | bytes accessed | tf_op | source)
XLA Modules:
  0.0 58.3 jit_solution(4054621346193579001)
XLA Ops:
  0.6 0.7 %pad_add_fusion.1 = (s32[2,4]{1,0:T(2,128)S(1)}, s32[2,4]{1,0:T(2,128)S(1)}) fusion(s32[1,4]{1,0:T(1,128)} %param.14, s32[1,4]{1,0:T(1,128)} %param.11), kind=kLoop, calls=%fused_computation.9 | loop fusion | flops 16 | bytes 96 | tf_op jit(solution)/shard_map/concatenate | solution.py:315
  1.3 0.1 select_reduce_fusion.2
  1.4 0.1 select_reduce_fusion.1
  1.5 0.7 %pad_add_fusion = (s32[2,192]{1,0:T(2,128)S(1)}, s32[2,192]{1,0:T(2,128)S(1)}) fusion(s32[1,192]{1,0:T(1,128)} %param.15, s32[1,192]{1,0:T(1,128)} %param.12, s32[2,192]{1,0:T(2,128)S(1)} %select_reduce_fusion.1), kind=kLoop, calls=%fused_computation.6 | loop fusion | flops 1152 | bytes 6144 | tf_op jit(solution)/shard_map/concatenate | solution.py:316
  2.2 0.2 select_reduce_fusion
  2.4 0.6 %broadcast_add_fusion.slots_ref = s32[2,768]{1,0:T(2,128)} fusion(s32[2,768]{1,0:T(2,128)S(1)} %select_reduce_fusion), kind=kLoop, calls=%fused_computation.5 | loop fusion | flops 1536 | bytes 12288 | tf_op jit(solution)/shard_map/add | solution.py:40
  3.0 52.4 %shard_map.95 = (bf16[3,6144]{1,0:T(4,128)(2,1)}, bf16[3,6144]{1,0:T(4,128)(2,1)}) custom-call(s32[2,768]{1,0:T(2,128)} %broadcast_add_fusion.slots_ref, bf16[3,6144]{1,0:T(4,128)(2,1)} %x_ref.1, bf16[3,6144]{1,0:T(4,128)(2,1)} %g_ref.1, bf16[1,52,4096]{2,1,0:T(8,128)(2,1)} %one_ref.1, bf16[1,52,4096]{2,1,0:T(8,128)(2,1)} %two_ref.1), custom_call_target="tpu_custom_call" | custom-call | tf_op jit(solution)/shard_map/pallas_call | solution.py:323
  55.4 1.4 %copy.12 = bf16[3,6144]{1,0:T(4,128)(2,1)} copy(bf16[3,6144]{1,0:T(4,128)(2,1)} %get-tuple-element.8) | data formatting | bytes 73728
  56.8 1.4 %copy.13 = bf16[3,6144]{1,0:T(4,128)(2,1)} copy(bf16[3,6144]{1,0:T(4,128)(2,1)} %get-tuple-element.9) | data formatting | bytes 73728
  (1 shorter events, 0.0 us)

commit v2 on v1

--- a/solution.py
+++ b/solution.py
@@ -10,6 +10,7 @@
 BS = 64
 HB_DEV = 8
 HALF = BS // 2
+PARTS = 3
 LANES = 128
 MESH = pl.DeviceIdType.MESH
 F32 = jnp.float32
@@ -63,17 +64,24 @@
     own_rows,
     got_x,
     got_g,
+    pair_x,
+    pair_g,
     spread,
     mat_x,
     mat_g,
-    send_out,
-    send_grad,
-    got_out,
-    got_grad,
+    sums_a,
+    sums_b,
+    pair_sums,
+    send_sums,
+    got_sums,
     tile_send,
     tile_recv,
     row_send,
     row_recv,
+    share_send,
+    share_recv,
+    join_send,
+    join_recv,
     sum_send,
     sum_recv,
 ):
@@ -83,11 +91,15 @@
     rows = own * n_seq
     chunk = own * groups
     width_blocks = width // BS
-    hid = HB_DEV * BS
+    mine = HB_DEV // 2
+    hid = mine * BS
+    part_groups = groups // PARTS
+    part_rows = rows * part_groups
     zero_slot = n_fsdp * capacity
     f = lax.axis_index("fsdp")
     s = lax.axis_index("seq")
-    pair = f + 1 - 2 * lax.rem(f, 2)
+    core = lax.rem(f, 2)
+    pair = f + 1 - 2 * core
     others = [lax.rem(f + 2 * j, n_fsdp) for j in range(1, n_fsdp // 2)]
     pair_others = [lax.rem(pair + 2 * j, n_fsdp) for j in range(1, n_fsdp // 2)]
     peers = [lax.rem(s + j, n_seq) for j in range(1, n_seq)]
@@ -128,13 +140,33 @@
             device_id_type=MESH,
         )
 
-    def sum_copy(which, source, got, owner, target, sem):
+    def sum_copy(turn, owner, target, sem):
         return pltpu.make_async_remote_copy(
-            src_ref=source.at[target],
-            dst_ref=got.at[owner],
-            send_sem=sum_send.at[which, sem],
-            recv_sem=sum_recv.at[which, owner],
+            src_ref=send_sums.at[turn, target],
+            dst_ref=got_sums.at[turn, owner],
+            send_sem=sum_send.at[turn, sem],
+            recv_sem=sum_recv.at[turn, owner],
             device_id=(f, target),
+            device_id_type=MESH,
+        )
+
+    def share_copy(which, source, target):
+        return pltpu.make_async_remote_copy(
+            src_ref=source,
+            dst_ref=target,
+            send_sem=share_send.at[which],
+            recv_sem=share_recv.at[which],
+            device_id=(pair, s),
+            device_id_type=MESH,
+        )
+
+    def join_copy(turn):
+        return pltpu.make_async_remote_copy(
+            src_ref=(sums_a, sums_b)[turn % 2].at[pl.ds(part_rows, part_rows)],
+            dst_ref=pair_sums.at[turn],
+            send_sem=join_send.at[turn],
+            recv_sem=join_recv.at[turn],
+            device_id=(pair, s),
             device_id_type=MESH,
         )
 
@@ -174,13 +206,20 @@
     got_x[s] = own_rows[0]
     got_g[s] = own_rows[1]
 
-    def collect_rows(which, got, mat):
+    def collect_rows(which, got, shared, mat):
         for peer in peers:
             row_copy(which, own_rows.at[which], got, peer, peer, 0).wait_recv()
-        spread[...] = got[...].reshape(n_seq * chunk, LANES).astype(F32)
-        for k in range(groups):
-            piece = spread[pl.ds(k, rows, stride=groups), :]
-            mat[:, k * LANES:(k + 1) * LANES] = piece.astype(BF16)
+        start(share_copy(which, got, shared))
+        for half, source in enumerate((got, shared)):
+            if half == 1:
+                share_copy(which, got, shared).wait_recv()
+            spread[...] = source[...].reshape(n_seq * chunk, LANES).astype(F32)
+            for k in range(groups):
+                piece = spread[pl.ds(k, rows, stride=groups), :]
+                mat[half, :, k * LANES:(k + 1) * LANES] = piece.astype(BF16)
+
+    def rows_of(mat, at):
+        return jnp.concatenate([mat[0, :, at], mat[1, :, at]], axis=0)
 
     def collect_tiles(which, buffer):
         for j, peer in enumerate(others):
@@ -197,25 +236,25 @@
         odd = jnp.concatenate([a[:, BS:], b[:, BS:]], axis=1)
         return jnp.concatenate([even, odd], axis=0)
 
-    collect_rows(0, got_x, mat_x)
+    collect_rows(0, got_x, pair_x, mat_x)
     collect_tiles(0, tiles_one)
 
     step = 4
 
     def build_first(i, total):
         for r in range(step):
-            block = (i * step + r) * HB_DEV
+            block = (i * step + r) * HB_DEV + core * mine
             at = pl.ds(pl.multiple_of((i * step + r) * BS, BS), BS)
-            for j in range(HB_DEV // 2):
+            for j in range(mine // 2):
                 tile = joined(
                     tiles_one, slots_ref[0, block + 2 * j], slots_ref[0, block + 2 * j + 1]
                 )
                 first[at, j * LANES:(j + 1) * LANES] = tile
         at = pl.ds(pl.multiple_of(i * (step * BS), step * BS), step * BS)
-        return total + jnp.dot(mat_x[:, at], first[at, :], preferred_element_type=F32)
+        return total + jnp.dot(rows_of(mat_x, at), first[at, :], preferred_element_type=F32)
 
     hidden = lax.fori_loop(
-        0, width_blocks // step, build_first, jnp.zeros((rows, hid), F32)
+        0, width_blocks // step, build_first, jnp.zeros((2 * rows, hid), F32)
     )
 
     def reorder(value, matrix):
@@ -231,64 +270,96 @@
     value, slope = gelu_pair(hidden)
     acts = value.astype(BF16)
 
-    collect_rows(1, got_g, mat_g)
+    collect_rows(1, got_g, pair_g, mat_g)
     collect_tiles(1, tiles_two)
 
-    def build_second(i, total):
+    def pass_on(turn):
+        join_copy(turn).wait_recv()
+        kept = (sums_a, sums_b)[turn % 2][0:part_rows, :]
+        total = (kept + pair_sums[turn]).astype(BF16)
+        send_sums[turn] = total.reshape(n_seq, own * part_groups, LANES)
+        for j, peer in enumerate(peers):
+            start(sum_copy(turn, s, peer, j))
+
+    pairs = part_groups // 2
+
+    def columns(part, i):
+        return pl.ds(pl.multiple_of((part * pairs + i) * 2 * LANES, 2 * LANES), 2 * LANES)
+
+    def put(turn, i, value):
+        target = (sums_a, sums_b)[turn % 2]
         for k in range(2):
-            block = i * 4 + 2 * k
-            at = pl.ds(pl.multiple_of((2 * i + k) * LANES, LANES), LANES)
-            for r in range(HB_DEV):
-                left = r * width_blocks + block
-                tile = joined(tiles_two, slots_ref[1, left], slots_ref[1, left + 1])
-                second[r * BS:(r + 1) * BS, at] = tile
-        at = pl.ds(pl.multiple_of(2 * i * LANES, 2 * LANES), 2 * LANES)
-        weight = second[:, at]
-        part = jnp.dot(acts, weight, preferred_element_type=F32)
-        for k in range(2):
-            spread[pl.ds(2 * i + k, rows, stride=groups), :] = part[:, k * LANES:(k + 1) * LANES]
-        return total + lax.dot_general(
-            mat_g[:, at], weight, (((1,), (1,)), ((), ())), preferred_element_type=F32
-        )
-
-    back = lax.fori_loop(0, groups // 2, build_second, jnp.zeros((rows, hid), F32))
-    send_out[...] = spread[...].astype(BF16).reshape(n_seq, chunk, LANES)
-    for j, peer in enumerate(peers):
-        start(sum_copy(0, send_out, got_out, s, peer, j))
+            at = pl.ds(2 * i + k, 2 * rows, stride=part_groups)
+            target[at, :] = value[:, k * LANES:(k + 1) * LANES]
+
+    back = jnp.zeros((2 * rows, hid), F32)
+    for turn in range(PARTS):
+        if turn >= 2:
+            join_copy(turn - 2).wait_send()
+
+        def build_second(i, total):
+            for k in range(2):
+                block = ((turn * pairs + i) * 2 + k) * 2
+                at = pl.ds(pl.multiple_of(block * BS, LANES), LANES)
+                for r in range(mine):
+                    left = (core * mine + r) * width_blocks + block
+                    tile = joined(tiles_two, slots_ref[1, left], slots_ref[1, left + 1])
+                    second[r * BS:(r + 1) * BS, at] = tile
+            at = columns(turn, i)
+            weight = second[:, at]
+            put(turn, i, jnp.dot(acts, weight, preferred_element_type=F32))
+            return total + lax.dot_general(
+                rows_of(mat_g, at),
+                weight,
+                (((1,), (1,)), ((), ())),
+                preferred_element_type=F32,
+            )
+
+        back = lax.fori_loop(0, pairs, build_second, back)
+        join_copy(turn).start()
+        if turn >= 1:
+            pass_on(turn - 1)
 
     pre = (back * slope).astype(BF16)
     pre = reorder(pre, from_halves).astype(BF16)
-
-    def in_grad(i, carry):
-        at = pl.ds(pl.multiple_of(2 * i * LANES, 2 * LANES), 2 * LANES)
-        part = lax.dot_general(
-            pre, first[at, :], (((1,), (1,)), ((), ())), preferred_element_type=F32
-        )
-        for k in range(2):
-            spread[pl.ds(2 * i + k, rows, stride=groups), :] = part[:, k * LANES:(k + 1) * LANES]
-        return carry
-
-    lax.fori_loop(0, groups // 2, in_grad, 0)
-    send_grad[...] = spread[...].astype(BF16).reshape(n_seq, chunk, LANES)
-    for j, peer in enumerate(peers):
-        start(sum_copy(1, send_grad, got_grad, s, peer, j))
-
-    def finish(which, source, got, target):
-        got[s] = source[s]
+    pass_on(PARTS - 1)
+
+    for turn in range(PARTS, 2 * PARTS):
+        join_copy(turn - 2).wait_send()
+
+        def in_grad(i, carry):
+            part = lax.dot_general(
+                pre,
+                first[columns(turn - PARTS, i), :],
+                (((1,), (1,)), ((), ())),
+                preferred_element_type=F32,
+            )
+            put(turn, i, part)
+            return carry
+
+        lax.fori_loop(0, pairs, in_grad, 0)
+        join_copy(turn).start()
+        if turn > PARTS:
+            pass_on(turn - 1)
+    pass_on(2 * PARTS - 1)
+
+    part_chunk = own * part_groups
+    for turn in range(2 * PARTS):
         for peer in peers:
-            sum_copy(which, source, got, peer, peer, 0).wait_recv()
-        total = lax.fori_loop(
-            0, n_seq, lambda i, t: t + got[i].astype(F32), jnp.zeros((chunk, LANES), F32)
-        )
-        if which == 1:
+            sum_copy(turn, peer, peer, 0).wait_recv()
+        total = send_sums[turn, s].astype(F32)
+        got_sums[turn, s] = jnp.zeros((part_chunk, LANES), BF16)
+        total = lax.fori_loop(0, n_seq, lambda i, t: t + got_sums[turn, i].astype(F32), total)
+        if turn >= PARTS:
             total = jnp.dot(total.astype(BF16), from_halves, preferred_element_type=F32)
-        stage[0:chunk, :] = total
-        for k in range(groups):
-            piece = stage[pl.ds(k, own, stride=groups), :]
-            target[:, k * LANES:(k + 1) * LANES] = piece.astype(BF16)
-
-    finish(0, send_out, got_out, out_ref)
-    finish(1, send_grad, got_grad, grad_ref)
+        stage[0:part_chunk, :] = total
+        target = out_ref if turn < PARTS else grad_ref
+        for k in range(part_groups):
+            piece = stage[pl.ds(k, own, stride=part_groups), :]
+            column = (turn % PARTS) * part_groups + k
+            target[:, column * LANES:(column + 1) * LANES] = piece.astype(BF16)
+    for turn in range(2 * PARTS - 2, 2 * PARTS):
+        join_copy(turn).wait_send()
     for copy in sent:
         copy.wait_send()
 
@@ -310,7 +381,8 @@
     width_blocks = width // BS
     rows = own * n_seq
     chunk = own * (width // LANES)
-    hid = HB_DEV * BS
+    hid = HB_DEV // 2 * BS
+    part = rows * (width // LANES) // PARTS
     table = block_slots(
         jnp.concatenate([first_count, second_count]),
         jnp.concatenate([first_blocks, second_blocks]),
@@ -337,19 +409,26 @@
             pltpu.VMEM((2, chunk, LANES), BF16),
             every,
             every,
-            pltpu.VMEM((n_seq * chunk, LANES), F32),
-            pltpu.VMEM((rows, width), BF16),
-            pltpu.VMEM((rows, width), BF16),
             every,
             every,
-            every,
-            every,
+            pltpu.VMEM((n_seq * chunk, LANES), F32),
+            pltpu.VMEM((2, rows, width), BF16),
+            pltpu.VMEM((2, rows, width), BF16),
+            pltpu.VMEM((2 * part, LANES), F32),
+            pltpu.VMEM((2 * part, LANES), F32),
+            pltpu.VMEM((2 * PARTS, part, LANES), F32),
+            pltpu.VMEM((2 * PARTS, n_seq, chunk // PARTS, LANES), BF16),
+            pltpu.VMEM((2 * PARTS, n_seq, chunk // PARTS, LANES), BF16),
             pltpu.SemaphoreType.DMA((2, n_fsdp + n_fsdp // 2)),
             pltpu.SemaphoreType.DMA((2, n_fsdp)),
             pltpu.SemaphoreType.DMA((2, n_seq)),
             pltpu.SemaphoreType.DMA((2, n_seq)),
-            pltpu.SemaphoreType.DMA((2, n_seq)),
-            pltpu.SemaphoreType.DMA((2, n_seq)),
+            pltpu.SemaphoreType.DMA((2,)),
+            pltpu.SemaphoreType.DMA((2,)),
+            pltpu.SemaphoreType.DMA((2 * PARTS,)),
+            pltpu.SemaphoreType.DMA((2 * PARTS,)),
+            pltpu.SemaphoreType.DMA((2 * PARTS, n_seq)),
+            pltpu.SemaphoreType.DMA((2 * PARTS, n_seq)),
         ],
         compiler_params=pltpu.CompilerParams(
             collective_id=0, has_side_effects=True, vmem_limit_bytes=56 * 1024 * 1024

time: 58.5 us -> 60.1 us (1.027)
  Pallas kernels: 52.4 us -> 54 us
    pallas_call x1, Pallas kernels: 52.4 us -> 54 us  [on_device(): pl.pallas_call(functools.partial(kernel, n_fsdp, n_seq), out_shape=(jax.S...]
where the time goes in v2:
time: 60.1 us; the launch traced here: 59.9 us
  Pallas kernels  54 us (90%)
  local copies, waits for them, and re-layouts  2.87 us (5%)
  other arithmetic  2.37 us (4%)
  between operations  0.65 us (1%)
    pallas_call x1, Pallas kernels, on_device(): pl.pallas_call(functools.partial(kernel, n_fsdp, n_seq), out_shape=(jax.S...  54 us
    unnamed x2, local copies, waits for them, and re-layouts  2.87 us

profile of v2, /device:TPU:0, one launch (start us, length us, event | category | flops | bytes accessed | tf_op | source)
XLA Modules:
  0.0 59.9 jit_solution(8781482328614801789)
XLA Ops:
  0.6 0.7 %pad_add_fusion.1 = (s32[2,4]{1,0:T(2,128)S(1)}, s32[2,4]{1,0:T(2,128)S(1)}) fusion(s32[1,4]{1,0:T(1,128)} %param.14, s32[1,4]{1,0:T(1,128)} %param.11), kind=kLoop, calls=%fused_computation.9 | loop fusion | flops 16 | bytes 96 | tf_op jit(solution)/shard_map/concatenate | solution.py:387
  1.3 0.1 select_reduce_fusion.2
  1.4 0.1 select_reduce_fusion.1
  1.5 0.7 %pad_add_fusion = (s32[2,192]{1,0:T(2,128)S(1)}, s32[2,192]{1,0:T(2,128)S(1)}) fusion(s32[1,192]{1,0:T(1,128)} %param.15, s32[1,192]{1,0:T(1,128)} %param.12, s32[2,192]{1,0:T(2,128)S(1)} %select_reduce_fusion.1), kind=kLoop, calls=%fused_computation.6 | loop fusion | flops 1152 | bytes 6144 | tf_op jit(solution)/shard_map/concatenate | solution.py:388
  2.2 0.2 select_reduce_fusion
  2.4 0.6 %broadcast_add_fusion.slots_ref = s32[2,768]{1,0:T(2,128)} fusion(s32[2,768]{1,0:T(2,128)S(1)} %select_reduce_fusion), kind=kLoop, calls=%fused_computation.5 | loop fusion | flops 1536 | bytes 12288 | tf_op jit(solution)/shard_map/add | solution.py:41
  3.0 54.0 %shard_map.95 = (bf16[3,6144]{1,0:T(4,128)(2,1)}, bf16[3,6144]{1,0:T(4,128)(2,1)}) custom-call(s32[2,768]{1,0:T(2,128)} %broadcast_add_fusion.slots_ref, bf16[3,6144]{1,0:T(4,128)(2,1)} %x_ref.1, bf16[3,6144]{1,0:T(4,128)(2,1)} %g_ref.1, bf16[1,52,4096]{2,1,0:T(8,128)(2,1)} %one_ref.1, bf16[1,52,4096]{2,1,0:T(8,128)(2,1)} %two_ref.1), custom_call_target="tpu_custom_call" | custom-call | tf_op jit(solution)/shard_map/pallas_call | solution.py:395
  57.0 1.4 %copy.12 = bf16[3,6144]{1,0:T(4,128)(2,1)} copy(bf16[3,6144]{1,0:T(4,128)(2,1)} %get-tuple-element.8) | data formatting | bytes 73728
  58.4 1.4 %copy.13 = bf16[3,6144]{1,0:T(4,128)(2,1)} copy(bf16[3,6144]{1,0:T(4,128)(2,1)} %get-tuple-element.9) | data formatting | bytes 73728
  (1 shorter events, 0.0 us)

commit v3 on v2

--- a/solution.py
+++ b/solution.py
@@ -61,7 +61,6 @@
     stage,
     first,
     second,
-    own_rows,
     got_x,
     got_g,
     pair_x,
@@ -73,6 +72,8 @@
     sums_b,
     pair_sums,
     send_sums,
+    half_sums,
+    both_sums,
     got_sums,
     tile_send,
     tile_recv,
@@ -82,6 +83,8 @@
     share_recv,
     join_send,
     join_recv,
+    half_send,
+    half_recv,
     sum_send,
     sum_recv,
 ):
@@ -102,12 +105,17 @@
     pair = f + 1 - 2 * core
     others = [lax.rem(f + 2 * j, n_fsdp) for j in range(1, n_fsdp // 2)]
     pair_others = [lax.rem(pair + 2 * j, n_fsdp) for j in range(1, n_fsdp // 2)]
-    peers = [lax.rem(s + j, n_seq) for j in range(1, n_seq)]
+    ranks = n_seq // 2
+    side = lax.rem(s, 2)
+    rank = s // 2
+    mate = s + 1 - 2 * side
+    far_ranks = [lax.rem(rank + j, ranks) for j in range(1, ranks)]
+    far = [2 * other + side for other in far_ranks]
 
     barrier = pltpu.get_barrier_semaphore()
     for peer in [pair] + others:
         pl.semaphore_signal(barrier, inc=1, device_id=(peer, s), device_id_type=MESH)
-    for peer in peers:
+    for peer in [mate] + far:
         pl.semaphore_signal(barrier, inc=1, device_id=(f, peer), device_id_type=MESH)
 
     def lay_tiles(source, target):
@@ -130,23 +138,36 @@
             device_id_type=MESH,
         )
 
-    def row_copy(which, source, got, owner, target, sem):
+    def place(owner_side, owner_rank):
+        return owner_side * ranks + owner_rank
+
+    def row_copy(which, got, slot, target, sem):
         return pltpu.make_async_remote_copy(
-            src_ref=source,
-            dst_ref=got.at[owner],
+            src_ref=got.at[slot],
+            dst_ref=got.at[slot],
             send_sem=row_send.at[which, sem],
-            recv_sem=row_recv.at[which, owner],
+            recv_sem=row_recv.at[which, slot],
             device_id=(f, target),
             device_id_type=MESH,
         )
 
+    def half_copy(turn):
+        return pltpu.make_async_remote_copy(
+            src_ref=send_sums.at[turn, pl.ds((1 - side) * ranks, ranks)],
+            dst_ref=half_sums.at[turn],
+            send_sem=half_send.at[turn],
+            recv_sem=half_recv.at[turn],
+            device_id=(f, mate),
+            device_id_type=MESH,
+        )
+
     def sum_copy(turn, owner, target, sem):
         return pltpu.make_async_remote_copy(
-            src_ref=send_sums.at[turn, target],
+            src_ref=both_sums.at[turn, target],
             dst_ref=got_sums.at[turn, owner],
             send_sem=sum_send.at[turn, sem],
             recv_sem=sum_recv.at[turn, owner],
-            device_id=(f, target),
+            device_id=(f, 2 * target + side),
             device_id_type=MESH,
         )
 
@@ -182,7 +203,7 @@
     from_halves = jnp.where(natural(row) == position, 1.0, 0.0).astype(BF16)
 
     lay_tiles(one_ref, tiles_one)
-    pl.semaphore_wait(barrier, 1 + len(others) + len(peers))
+    pl.semaphore_wait(barrier, 2 + len(others) + len(far))
     for j, peer in enumerate(others):
         start(tile_copy(0, tiles_one, f, peer, j))
 
@@ -192,23 +213,31 @@
             stage[pl.ds(k, own, stride=groups), :] = piece
         return stage[0:chunk, :].astype(BF16)
 
-    own_rows[0] = jnp.dot(lay_rows(x_ref), to_halves, preferred_element_type=F32).astype(BF16)
-    for j, peer in enumerate(peers):
-        start(row_copy(0, own_rows.at[0], got_x, s, peer, j))
+    here = place(side, rank)
+
+    def send_rows(which, got):
+        for j, peer in enumerate(far):
+            start(row_copy(which, got, here, peer, j))
+        start(row_copy(which, got, here, mate, ranks))
+
+    def relay_rows(which, got):
+        for j, other in enumerate(far_ranks):
+            row_copy(which, got, place(side, other), mate, 0).wait_recv()
+            start(row_copy(which, got, place(side, other), mate, ranks + 1 + j))
+
+    got_x[here] = jnp.dot(lay_rows(x_ref), to_halves, preferred_element_type=F32).astype(BF16)
+    send_rows(0, got_x)
     start(tile_copy(0, tiles_one, f, pair, n_fsdp))
     lay_tiles(two_ref, tiles_two)
     for j, peer in enumerate(others):
         start(tile_copy(1, tiles_two, f, peer, j))
-    own_rows[1] = lay_rows(g_ref)
-    for j, peer in enumerate(peers):
-        start(row_copy(1, own_rows.at[1], got_g, s, peer, j))
+    got_g[here] = lay_rows(g_ref)
+    send_rows(1, got_g)
     start(tile_copy(1, tiles_two, f, pair, n_fsdp))
-    got_x[s] = own_rows[0]
-    got_g[s] = own_rows[1]
 
     def collect_rows(which, got, shared, mat):
-        for peer in peers:
-            row_copy(which, own_rows.at[which], got, peer, peer, 0).wait_recv()
+        for other in [rank] + far_ranks:
+            row_copy(which, got, place(1 - side, other), mate, 0).wait_recv()
         start(share_copy(which, got, shared))
         for half, source in enumerate((got, shared)):
             if half == 1:
@@ -236,6 +265,8 @@
         odd = jnp.concatenate([a[:, BS:], b[:, BS:]], axis=1)
         return jnp.concatenate([even, odd], axis=0)
 
+    relay_rows(0, got_x)
+    relay_rows(1, got_g)
     collect_rows(0, got_x, pair_x, mat_x)
     collect_tiles(0, tiles_one)
 
@@ -278,8 +309,14 @@
         kept = (sums_a, sums_b)[turn % 2][0:part_rows, :]
         total = (kept + pair_sums[turn]).astype(BF16)
         send_sums[turn] = total.reshape(n_seq, own * part_groups, LANES)
-        for j, peer in enumerate(peers):
-            start(sum_copy(turn, s, peer, j))
+        start(half_copy(turn))
+
+    def spread_sums(turn):
+        half_copy(turn).wait_recv()
+        kept = send_sums[turn, pl.ds(side * ranks, ranks)].astype(F32)
+        both_sums[turn] = (kept + half_sums[turn].astype(F32)).astype(BF16)
+        for j, other in enumerate(far_ranks):
+            start(sum_copy(turn, rank, other, j))
 
     pairs = part_groups // 2
 
@@ -319,10 +356,13 @@
         join_copy(turn).start()
         if turn >= 1:
             pass_on(turn - 1)
+        if turn >= 2:
+            spread_sums(turn - 2)
 
     pre = (back * slope).astype(BF16)
     pre = reorder(pre, from_halves).astype(BF16)
     pass_on(PARTS - 1)
+    spread_sums(PARTS - 2)
 
     for turn in range(PARTS, 2 * PARTS):
         join_copy(turn - 2).wait_send()
@@ -341,15 +381,17 @@
         join_copy(turn).start()
         if turn > PARTS:
             pass_on(turn - 1)
+            spread_sums(turn - 2)
     pass_on(2 * PARTS - 1)
+    spread_sums(2 * PARTS - 2)
+    spread_sums(2 * PARTS - 1)
 
     part_chunk = own * part_groups
     for turn in range(2 * PARTS):
-        for peer in peers:
-            sum_copy(turn, peer, peer, 0).wait_recv()
-        total = send_sums[turn, s].astype(F32)
-        got_sums[turn, s] = jnp.zeros((part_chunk, LANES), BF16)
-        total = lax.fori_loop(0, n_seq, lambda i, t: t + got_sums[turn, i].astype(F32), total)
+        total = both_sums[turn, rank].astype(F32)
+        for other in far_ranks:
+            sum_copy(turn, other, other, 0).wait_recv()
+            total = total + got_sums[turn, other].astype(F32)
         if turn >= PARTS:
             total = jnp.dot(total.astype(BF16), from_halves, preferred_element_type=F32)
         stage[0:part_chunk, :] = total
@@ -391,6 +433,7 @@
     )
     vmem = pl.BlockSpec(memory_space=pltpu.VMEM)
     bank = pltpu.VMEM((n_fsdp * capacity + 1, HALF, LANES), BF16)
+    some = pltpu.VMEM((2 * PARTS, n_seq // 2, chunk // PARTS, LANES), BF16)
     every = pltpu.VMEM((n_seq, chunk, LANES), BF16)
     return pl.pallas_call(
         functools.partial(kernel, n_fsdp, n_seq),
@@ -406,7 +449,6 @@
             pltpu.VMEM((max(capacity * HALF, chunk), LANES), F32),
             pltpu.VMEM((width, hid), BF16),
             pltpu.VMEM((hid, width), BF16),
-            pltpu.VMEM((2, chunk, LANES), BF16),
             every,
             every,
             every,
@@ -418,7 +460,9 @@
             pltpu.VMEM((2 * part, LANES), F32),
             pltpu.VMEM((2 * PARTS, part, LANES), F32),
             pltpu.VMEM((2 * PARTS, n_seq, chunk // PARTS, LANES), BF16),
-            pltpu.VMEM((2 * PARTS, n_seq, chunk // PARTS, LANES), BF16),
+            some,
+            some,
+            some,
             pltpu.SemaphoreType.DMA((2, n_fsdp + n_fsdp // 2)),
             pltpu.SemaphoreType.DMA((2, n_fsdp)),
             pltpu.SemaphoreType.DMA((2, n_seq)),
@@ -427,8 +471,10 @@
             pltpu.SemaphoreType.DMA((2,)),
             pltpu.SemaphoreType.DMA((2 * PARTS,)),
             pltpu.SemaphoreType.DMA((2 * PARTS,)),
-            pltpu.SemaphoreType.DMA((2 * PARTS, n_seq)),
-            pltpu.SemaphoreType.DMA((2 * PARTS, n_seq)),
+            pltpu.SemaphoreType.DMA((2 * PARTS,)),
+            pltpu.SemaphoreType.DMA((2 * PARTS,)),
+            pltpu.SemaphoreType.DMA((2 * PARTS, n_seq // 2)),
+            pltpu.SemaphoreType.DMA((2 * PARTS, n_seq // 2)),
         ],
         compiler_params=pltpu.CompilerParams(
             collective_id=0, has_side_effects=True, vmem_limit_bytes=56 * 1024 * 1024

time: 60.1 us -> 61.4 us (1.022)
  Pallas kernels: 54 us -> 55.2 us
    pallas_call x1, Pallas kernels: 54 us -> 55.2 us  [on_device(): pl.pallas_call(functools.partial(kernel, n_fsdp, n_seq), out_shape=(jax.S...]
where the time goes in v3:
time: 61.4 us; the launch traced here: 61.1 us
  Pallas kernels  55.2 us (90%)
  local copies, waits for them, and re-layouts  2.87 us (5%)
  other arithmetic  2.37 us (4%)
  between operations  0.65 us (1%)
    pallas_call x1, Pallas kernels, on_device(): pl.pallas_call(functools.partial(kernel, n_fsdp, n_seq), out_shape=(jax.S...  55.2 us
    unnamed x2, local copies, waits for them, and re-layouts  2.87 us

profile of v3, /device:TPU:0, one launch (start us, length us, event | category | flops | bytes accessed | tf_op | source)
XLA Modules:
  0.0 61.1 jit_solution(6368016138554097724)
XLA Ops:
  0.6 0.7 %pad_add_fusion.1 = (s32[2,4]{1,0:T(2,128)S(1)}, s32[2,4]{1,0:T(2,128)S(1)}) fusion(s32[1,4]{1,0:T(1,128)} %param.14, s32[1,4]{1,0:T(1,128)} %param.11), kind=kLoop, calls=%fused_computation.9 | loop fusion | flops 16 | bytes 96 | tf_op jit(solution)/shard_map/concatenate | solution.py:429
  1.3 0.1 select_reduce_fusion.2
  1.4 0.1 select_reduce_fusion.1
  1.5 0.7 %pad_add_fusion = (s32[2,192]{1,0:T(2,128)S(1)}, s32[2,192]{1,0:T(2,128)S(1)}) fusion(s32[1,192]{1,0:T(1,128)} %param.15, s32[1,192]{1,0:T(1,128)} %param.12, s32[2,192]{1,0:T(2,128)S(1)} %select_reduce_fusion.1), kind=kLoop, calls=%fused_computation.6 | loop fusion | flops 1152 | bytes 6144 | tf_op jit(solution)/shard_map/concatenate | solution.py:430
  2.2 0.2 select_reduce_fusion
  2.4 0.6 broadcast_add_fusion.slots_ref
  3.0 55.2 %shard_map.95 = (bf16[3,6144]{1,0:T(4,128)(2,1)}, bf16[3,6144]{1,0:T(4,128)(2,1)}) custom-call(s32[2,768]{1,0:T(2,128)} %broadcast_add_fusion.slots_ref, bf16[3,6144]{1,0:T(4,128)(2,1)} %x_ref.1, bf16[3,6144]{1,0:T(4,128)(2,1)} %g_ref.1, bf16[1,52,4096]{2,1,0:T(8,128)(2,1)} %one_ref.1, bf16[1,52,4096]{2,1,0:T(8,128)(2,1)} %two_ref.1), custom_call_target="tpu_custom_call" | custom-call | tf_op jit(solution)/shard_map/pallas_call | solution.py:438
  58.2 1.4 %copy.12 = bf16[3,6144]{1,0:T(4,128)(2,1)} copy(bf16[3,6144]{1,0:T(4,128)(2,1)} %get-tuple-element.8) | data formatting | bytes 73728
  59.7 1.4 %copy.13 = bf16[3,6144]{1,0:T(4,128)(2,1)} copy(bf16[3,6144]{1,0:T(4,128)(2,1)} %get-tuple-element.9) | data formatting | bytes 73728
  (1 shorter events, 0.0 us)

commit v4 on v1

--- a/solution.py
+++ b/solution.py
@@ -10,6 +10,7 @@
 BS = 64
 HB_DEV = 8
 HALF = BS // 2
+PARTS = 3
 LANES = 128
 MESH = pl.DeviceIdType.MESH
 F32 = jnp.float32
@@ -66,10 +67,8 @@
     spread,
     mat_x,
     mat_g,
-    send_out,
-    send_grad,
-    got_out,
-    got_grad,
+    send_sums,
+    got_sums,
     tile_send,
     tile_recv,
     row_send,
@@ -84,6 +83,10 @@
     chunk = own * groups
     width_blocks = width // BS
     hid = HB_DEV * BS
+    part_groups = groups // PARTS
+    part_chunk = own * part_groups
+    part_rows = rows * part_groups
+    pairs = part_groups // 2
     zero_slot = n_fsdp * capacity
     f = lax.axis_index("fsdp")
     s = lax.axis_index("seq")
@@ -128,12 +131,12 @@
             device_id_type=MESH,
         )
 
-    def sum_copy(which, source, got, owner, target, sem):
+    def sum_copy(turn, owner, target, sem):
         return pltpu.make_async_remote_copy(
-            src_ref=source.at[target],
-            dst_ref=got.at[owner],
-            send_sem=sum_send.at[which, sem],
-            recv_sem=sum_recv.at[which, owner],
+            src_ref=send_sums.at[turn, target],
+            dst_ref=got_sums.at[turn, owner],
+            send_sem=sum_send.at[turn, sem],
+            recv_sem=sum_recv.at[turn, owner],
             device_id=(f, target),
             device_id_type=MESH,
         )
@@ -182,10 +185,12 @@
             piece = spread[pl.ds(k, rows, stride=groups), :]
             mat[:, k * LANES:(k + 1) * LANES] = piece.astype(BF16)
 
-    def collect_tiles(which, buffer):
+    def relay_tiles(which, buffer):
         for j, peer in enumerate(others):
             tile_copy(which, buffer, peer, pair, 0).wait_recv()
             start(tile_copy(which, buffer, peer, pair, n_fsdp + 1 + j))
+
+    def collect_tiles(which, buffer):
         tile_copy(which, buffer, pair, pair, 0).wait_recv()
         for peer in pair_others:
             tile_copy(which, buffer, peer, pair, 0).wait_recv()
@@ -198,6 +203,7 @@
         return jnp.concatenate([even, odd], axis=0)
 
     collect_rows(0, got_x, mat_x)
+    relay_tiles(0, tiles_one)
     collect_tiles(0, tiles_one)
 
     step = 4
@@ -231,64 +237,73 @@
     value, slope = gelu_pair(hidden)
     acts = value.astype(BF16)
 
+    relay_tiles(1, tiles_two)
     collect_rows(1, got_g, mat_g)
     collect_tiles(1, tiles_two)
 
-    def build_second(i, total):
+    def put(i, value):
         for k in range(2):
-            block = i * 4 + 2 * k
-            at = pl.ds(pl.multiple_of((2 * i + k) * LANES, LANES), LANES)
-            for r in range(HB_DEV):
-                left = r * width_blocks + block
-                tile = joined(tiles_two, slots_ref[1, left], slots_ref[1, left + 1])
-                second[r * BS:(r + 1) * BS, at] = tile
-        at = pl.ds(pl.multiple_of(2 * i * LANES, 2 * LANES), 2 * LANES)
-        weight = second[:, at]
-        part = jnp.dot(acts, weight, preferred_element_type=F32)
-        for k in range(2):
-            spread[pl.ds(2 * i + k, rows, stride=groups), :] = part[:, k * LANES:(k + 1) * LANES]
-        return total + lax.dot_general(
-            mat_g[:, at], weight, (((1,), (1,)), ((), ())), preferred_element_type=F32
-        )
-
-    back = lax.fori_loop(0, groups // 2, build_second, jnp.zeros((rows, hid), F32))
-    send_out[...] = spread[...].astype(BF16).reshape(n_seq, chunk, LANES)
-    for j, peer in enumerate(peers):
-        start(sum_copy(0, send_out, got_out, s, peer, j))
+            at = pl.ds(2 * i + k, rows, stride=part_groups)
+            spread[at, :] = value[:, k * LANES:(k + 1) * LANES]
+
+    def send_part(turn):
+        total = spread[0:part_rows, :].astype(BF16)
+        send_sums[turn] = total.reshape(n_seq, part_chunk, LANES)
+        for j, peer in enumerate(peers):
+            start(sum_copy(turn, s, peer, j))
+
+    back = jnp.zeros((rows, hid), F32)
+    for turn in range(PARTS):
+
+        def build_second(i, total):
+            n = turn * pairs + i
+            for k in range(2):
+                block = n * 4 + 2 * k
+                at = pl.ds(pl.multiple_of((2 * n + k) * LANES, LANES), LANES)
+                for r in range(HB_DEV):
+                    left = r * width_blocks + block
+                    tile = joined(tiles_two, slots_ref[1, left], slots_ref[1, left + 1])
+                    second[r * BS:(r + 1) * BS, at] = tile
+            at = pl.ds(pl.multiple_of(2 * n * LANES, 2 * LANES), 2 * LANES)
+            weight = second[:, at]
+            put(i, jnp.dot(acts, weight, preferred_element_type=F32))
+            return total + lax.dot_general(
+                mat_g[:, at], weight, (((1,), (1,)), ((), ())), preferred_element_type=F32
+            )
+
+        back = lax.fori_loop(0, pairs, build_second, back)
+        send_part(turn)
 
     pre = (back * slope).astype(BF16)
     pre = reorder(pre, from_halves).astype(BF16)
 
-    def in_grad(i, carry):
-        at = pl.ds(pl.multiple_of(2 * i * LANES, 2 * LANES), 2 * LANES)
-        part = lax.dot_general(
-            pre, first[at, :], (((1,), (1,)), ((), ())), preferred_element_type=F32
-        )
-        for k in range(2):
-            spread[pl.ds(2 * i + k, rows, stride=groups), :] = part[:, k * LANES:(k + 1) * LANES]
-        return carry
-
-    lax.fori_loop(0, groups // 2, in_grad, 0)
-    send_grad[...] = spread[...].astype(BF16).reshape(n_seq, chunk, LANES)
-    for j, peer in enumerate(peers):
-        start(sum_copy(1, send_grad, got_grad, s, peer, j))
-
-    def finish(which, source, got, target):
-        got[s] = source[s]
+    for turn in range(PARTS, 2 * PARTS):
+
+        def in_grad(i, carry):
+            n = (turn - PARTS) * pairs + i
+            at = pl.ds(pl.multiple_of(2 * n * LANES, 2 * LANES), 2 * LANES)
+            part = lax.dot_general(
+                pre, first[at, :], (((1,), (1,)), ((), ())), preferred_element_type=F32
+            )
+            put(i, part)
+            return carry
+
+        lax.fori_loop(0, pairs, in_grad, 0)
+        send_part(turn)
+
+    for turn in range(2 * PARTS):
+        total = send_sums[turn, s].astype(F32)
         for peer in peers:
-            sum_copy(which, source, got, peer, peer, 0).wait_recv()
-        total = lax.fori_loop(
-            0, n_seq, lambda i, t: t + got[i].astype(F32), jnp.zeros((chunk, LANES), F32)
-        )
-        if which == 1:
+            sum_copy(turn, peer, peer, 0).wait_recv()
+            total = total + got_sums[turn, peer].astype(F32)
+        if turn >= PARTS:
             total = jnp.dot(total.astype(BF16), from_halves, preferred_element_type=F32)
-        stage[0:chunk, :] = total
-        for k in range(groups):
-            piece = stage[pl.ds(k, own, stride=groups), :]
-            target[:, k * LANES:(k + 1) * LANES] = piece.astype(BF16)
-
-    finish(0, send_out, got_out, out_ref)
-    finish(1, send_grad, got_grad, grad_ref)
+        stage[0:part_chunk, :] = total
+        target = out_ref if turn < PARTS else grad_ref
+        for k in range(part_groups):
+            piece = stage[pl.ds(k, own, stride=part_groups), :]
+            column = (turn % PARTS) * part_groups + k
+            target[:, column * LANES:(column + 1) * LANES] = piece.astype(BF16)
     for copy in sent:
         copy.wait_send()
 
@@ -319,6 +334,7 @@
     )
     vmem = pl.BlockSpec(memory_space=pltpu.VMEM)
     bank = pltpu.VMEM((n_fsdp * capacity + 1, HALF, LANES), BF16)
+    parts = pltpu.VMEM((2 * PARTS, n_seq, chunk // PARTS, LANES), BF16)
     every = pltpu.VMEM((n_seq, chunk, LANES), BF16)
     return pl.pallas_call(
         functools.partial(kernel, n_fsdp, n_seq),
@@ -340,16 +356,14 @@
             pltpu.VMEM((n_seq * chunk, LANES), F32),
             pltpu.VMEM((rows, width), BF16),
             pltpu.VMEM((rows, width), BF16),
-            every,
-            every,
-            every,
-            every,
+            parts,
+            parts,
             pltpu.SemaphoreType.DMA((2, n_fsdp + n_fsdp // 2)),
             pltpu.SemaphoreType.DMA((2, n_fsdp)),
             pltpu.SemaphoreType.DMA((2, n_seq)),
             pltpu.SemaphoreType.DMA((2, n_seq)),
-            pltpu.SemaphoreType.DMA((2, n_seq)),
-            pltpu.SemaphoreType.DMA((2, n_seq)),
+            pltpu.SemaphoreType.DMA((2 * PARTS, n_seq)),
+            pltpu.SemaphoreType.DMA((2 * PARTS, n_seq)),
         ],
         compiler_params=pltpu.CompilerParams(
             collective_id=0, has_side_effects=True, vmem_limit_bytes=56 * 1024 * 1024

time: 58.5 us -> 57.7 us (0.986)
  Pallas kernels: 52.4 us -> 51.5 us
    pallas_call x1, Pallas kernels: 52.4 us -> 51.5 us  [on_device(): pl.pallas_call(functools.partial(kernel, n_fsdp, n_seq), out_shape=(jax.S...]
where the time goes in v4:
time: 57.7 us; the launch traced here: 57.4 us
  Pallas kernels  51.5 us (89%)
  local copies, waits for them, and re-layouts  2.87 us (5%)
  other arithmetic  2.37 us (4%)
  between operations  0.65 us (1%)
    pallas_call x1, Pallas kernels, on_device(): pl.pallas_call(functools.partial(kernel, n_fsdp, n_seq), out_shape=(jax.S...  51.5 us
    unnamed x2, local copies, waits for them, and re-layouts  2.87 us

profile of v4, /device:TPU:0, one launch (start us, length us, event | category | flops | bytes accessed | tf_op | source)
XLA Modules:
  0.0 57.4 jit_solution(1266789236420630479)
XLA Ops:
  0.6 0.7 %pad_add_fusion.1 = (s32[2,4]{1,0:T(2,128)S(1)}, s32[2,4]{1,0:T(2,128)S(1)}) fusion(s32[1,4]{1,0:T(1,128)} %param.14, s32[1,4]{1,0:T(1,128)} %param.11), kind=kLoop, calls=%fused_computation.9 | loop fusion | flops 16 | bytes 96 | tf_op jit(solution)/shard_map/concatenate | solution.py:330
  1.3 0.1 select_reduce_fusion.2
  1.4 0.1 select_reduce_fusion.1
  1.5 0.7 %pad_add_fusion = (s32[2,192]{1,0:T(2,128)S(1)}, s32[2,192]{1,0:T(2,128)S(1)}) fusion(s32[1,192]{1,0:T(1,128)} %param.15, s32[1,192]{1,0:T(1,128)} %param.12, s32[2,192]{1,0:T(2,128)S(1)} %select_reduce_fusion.1), kind=kLoop, calls=%fused_computation.6 | loop fusion | flops 1152 | bytes 6144 | tf_op jit(solution)/shard_map/concatenate | solution.py:331
  2.2 0.2 select_reduce_fusion
  2.4 0.6 %broadcast_add_fusion.slots_ref = s32[2,768]{1,0:T(2,128)} fusion(s32[2,768]{1,0:T(2,128)S(1)} %select_reduce_fusion), kind=kLoop, calls=%fused_computation.5 | loop fusion | flops 1536 | bytes 12288 | tf_op jit(solution)/shard_map/add | solution.py:41
  3.0 51.5 %shard_map.95 = (bf16[3,6144]{1,0:T(4,128)(2,1)}, bf16[3,6144]{1,0:T(4,128)(2,1)}) custom-call(s32[2,768]{1,0:T(2,128)} %broadcast_add_fusion.slots_ref, bf16[3,6144]{1,0:T(4,128)(2,1)} %x_ref.1, bf16[3,6144]{1,0:T(4,128)(2,1)} %g_ref.1, bf16[1,52,4096]{2,1,0:T(8,128)(2,1)} %one_ref.1, bf16[1,52,4096]{2,1,0:T(8,128)(2,1)} %two_ref.1), custom_call_target="tpu_custom_call" | custom-call | tf_op jit(solution)/shard_map/pallas_call | solution.py:339
  54.6 1.4 %copy.12 = bf16[3,6144]{1,0:T(4,128)(2,1)} copy(bf16[3,6144]{1,0:T(4,128)(2,1)} %get-tuple-element.8) | data formatting | bytes 73728
  56.0 1.4 %copy.13 = bf16[3,6144]{1,0:T(4,128)(2,1)} copy(bf16[3,6144]{1,0:T(4,128)(2,1)} %get-tuple-element.9) | data formatting | bytes 73728
  (1 shorter events, 0.0 us)
